TPU v7x, 32 devices: a whole 2x2x4 slice. The times are simulated.
32 devices in a mesh: section: 2 (over y), dp: 16 (over z, x, core).
Axes of the slice: x: 2, y: 2, z: 4, core: 2. Of those that a mesh axis runs over, the one named last changes fastest.
Arguments:
- queries: bfloat16 [2, 2048, 2560], P('section', 'dp')
- key_cells: bfloat16 [2, 2048, 2560], P('section', 'dp')
- value_cells: bfloat16 [2, 2048, 2560], P('section', 'dp'), may hold values from -6 to 6
- grad_cells: bfloat16 [2, 2048, 2560], P('section', 'dp'), may hold values from -6 to 6
- packing: int32 [2, 16, 128], P('section', 'dp'), may hold values from 0 to 127, each once within a row
- segment_ids: int32 [2, 2048], P('section'), may hold values from 0 to 127, never falling along the last dimension, each value on 1 to 32 neighbouring positions
Outputs:
- input_grads: bfloat16 [2, 2048, 7680], P('section', 'dp')
Inputs may be any that keep to these rules, and one draw needn't show every extreme that they name: `packing`: each row of a section and device is a permutation of 0 to 127. `segment_ids`: along a section's packed cells the ids never fall; each segment has 1 to 32 cells and one has exactly 32.
All inputs are finite; a program needn't handle non-finite values.
Results may differ from a plain program's by a relative error of at most 0.0086.
Values may be sent and summed in bfloat16 or wider, within the bound.
A program may use at most 64 MiB of HBM per device.

v0:
```python
import functools
import jax
import jax.numpy as jnp
from jax import lax
from jax.sharding import PartitionSpec as P
from jax.experimental import pallas as pl
from jax.experimental.pallas import tpu as pltpu

HEADS = 20
HEAD_DIM = 128
CHUNK = 256
MESH = pl.DeviceIdType.MESH
NEG = -1e30
GROUPS = 12
INNER, TURN = 40, 32


def with_halo(value, sides, width):
    for axis, dim in sides:
        size, length = (lax.axis_size(axis), value.shape[dim])
        up = [(i, (i + 1) % size) for i in range(size - 1)]
        down = [(j, i) for i, j in up]
        last = lax.slice_in_dim(value, length - width, length, axis=dim)
        initial = lax.slice_in_dim(value, 0, width, axis=dim)
        before = lax.ppermute(last, axis, up)
        after = lax.ppermute(initial, axis, down)
        value = jnp.concatenate([before, value, after], axis=dim)
    return value


def passed_along(value, axis, steps):
    count = lax.axis_size(axis)
    initial, last = (max(0, -steps), min(count, count - steps))
    return lax.ppermute(value, axis, [(source, source + steps) for source in range(initial, last)])


def from_behind(block, axis, distance):
    devices = range(lax.axis_size(axis))
    route = [((i - distance) % len(devices), i) for i in devices]
    return lax.ppermute(block, axis, route)


def heads_of(matrix):
    return matrix.reshape(matrix.shape[0], HEADS, HEAD_DIM)


def masked_scores(query_rows, key_rows, query_ids, key_ids):
    scores = jnp.einsum(
        "ihd,jhd->hij", heads_of(query_rows), heads_of(key_rows), preferred_element_type=jnp.float32
    )
    scores = scores * HEAD_DIM ** (-0.5)
    allowed = (query_ids[:, None] == key_ids[None, :])[None]
    return jnp.where(allowed, scores, -jnp.inf)


def body(queries, key_cells, value_cells, grad_cells, packing, segment_ids):
    cell_count = queries.shape[1]
    width = queries.shape[2]
    groups = lax.axis_size("dp")
    per_peer = cell_count // groups
    reach = cell_count // 4
    place = lax.axis_index("dp")
    scale = HEAD_DIM ** (-0.5)
    order = packing[0, 0]

    def pack(matrix):
        return matrix[0][order].reshape(groups, per_peer, width)

    arrived = (
        lax.all_to_all(pack(queries), "dp", split_axis=0, concat_axis=0, tiled=True),
        lax.all_to_all(pack(key_cells), "dp", split_axis=0, concat_axis=0, tiled=True),
        lax.all_to_all(pack(value_cells), "dp", split_axis=0, concat_axis=0, tiled=True),
        lax.all_to_all(pack(grad_cells), "dp", split_axis=0, concat_axis=0, tiled=True),
    )
    own_q, own_k, own_v, own_g = [piece.reshape(cell_count, width) for piece in arrived]
    rim_ids = jnp.full((reach,), -1, jnp.int32)
    padded_ids = jnp.concatenate([rim_ids, segment_ids[0], rim_ids])
    window_ids = lax.dynamic_slice_in_dim(padded_ids, place * cell_count, cell_count + 2 * reach)
    own_ids = window_ids[reach : reach + cell_count]
    key_value = jnp.concatenate([own_k, own_v], axis=1)
    key_value_window = with_halo(key_value, (("dp", 0),), reach)
    key_window = key_value_window[:, :width]
    value_window = key_value_window[:, width:]
    scores = masked_scores(own_q, key_window, own_ids, window_ids)
    top = jnp.max(scores, axis=2)
    log_total = top + jnp.log(jnp.sum(jnp.exp(scores - top[:, :, None]), axis=2))
    probs = jnp.exp(scores - log_total[:, :, None])
    probs_low = probs.astype(jnp.bfloat16)
    grad_heads = heads_of(own_g)
    attended = jnp.einsum(
        "hij,jhd->ihd", probs_low, heads_of(value_window), preferred_element_type=jnp.float32
    )
    delta = jnp.sum(grad_heads.astype(jnp.float32) * attended, axis=2).T
    dprobs = jnp.einsum(
        "ihd,jhd->hij", grad_heads, heads_of(value_window), preferred_element_type=jnp.float32
    )
    dscores = (probs * (dprobs - delta[:, :, None]) * scale).astype(jnp.bfloat16)
    grad_query = jnp.einsum(
        "hij,jhd->ihd", dscores, heads_of(key_window), preferred_element_type=jnp.float32
    )
    grad_query = grad_query.reshape(cell_count, width).astype(jnp.bfloat16)
    window = cell_count + 2 * reach
    grad_key = jnp.einsum(
        "hij,ihd->jhd", dscores, heads_of(own_q), preferred_element_type=jnp.float32
    )
    grad_value = jnp.einsum(
        "hij,ihd->jhd", probs_low, grad_heads, preferred_element_type=jnp.float32
    )
    partial_value = jnp.concatenate(
        [grad_key.reshape(window, width), grad_value.reshape(window, width)], axis=1
    )
    from_after = passed_along(partial_value[:reach].astype(jnp.bfloat16), "dp", -1).astype(
        jnp.float32
    )
    from_before = passed_along(
        partial_value[reach + cell_count :].astype(jnp.bfloat16), "dp", 1
    ).astype(jnp.float32)
    summed = partial_value[reach : reach + cell_count]
    summed = summed.at[cell_count - reach :].add(from_after)
    summed = summed.at[:reach].add(from_before)
    packed_grads = jnp.concatenate([grad_query, summed.astype(jnp.bfloat16)], axis=1)
    returned = lax.all_to_all(
        packed_grads.reshape(groups, per_peer, 3 * width),
        "dp",
        split_axis=0,
        concat_axis=0,
        tiled=True,
    )
    returned = returned.reshape(cell_count, 3 * width)
    inverse = (
        jnp.zeros((cell_count,), jnp.int32).at[order].set(jnp.arange(cell_count, dtype=jnp.int32))
    )
    loaded_order = returned[inverse]
    handed = from_behind(loaded_order, "section", -1)
    return handed[None]


def dot_nt(a, b):
    return lax.dot_general(a, b, (((1,), (1,)), ((), ())), preferred_element_type=jnp.float32)


def dot_tn(a, b):
    return lax.dot_general(a, b, (((0,), (0,)), ((), ())), preferred_element_type=jnp.float32)


def dot_nn(a, b):
    return jnp.dot(a, b, preferred_element_type=jnp.float32)


def one_hot(index, dim, shape):
    return jnp.where(lax.broadcasted_iota(jnp.int32, shape, dim) == index, 1.0, 0.0).astype(jnp.bfloat16)


def small(x):
    return x.astype(jnp.float32).astype(jnp.bfloat16)


def upright(row):
    eye = one_hot(lax.broadcasted_iota(jnp.int32, (1, 128), 1), 0, (128, 128))
    column = dot_nt(eye, small(jnp.broadcast_to(row, (16, 128))))
    return column[:, 0:1].astype(jnp.int32)


def directions(tails, heads, turn):
    subset = lax.broadcasted_iota(jnp.int32, (4, 128), 1)
    number = lax.broadcasted_iota(jnp.int32, (4, 128), 0)
    chosen = jnp.where(number == 0, subset, jnp.where(number == 1, subset // 2, subset // 4))
    chosen = jnp.where(number == 3, subset // 8, chosen) % 2
    right, left = chosen * tails, (1 - chosen) * heads

    def total(x, rows):
        return sum(x[i : i + 1] for i in rows)

    inner = (total(right, range(4)) <= INNER) & (total(left, range(4)) <= INNER)
    turned = (total(right, range(3)) <= TURN) & (total(left, range(3)) <= TURN)
    turned = turned & (right[3:4] <= 16) & (left[3:4] <= 16)
    fits = jnp.where(turn, turned.astype(jnp.int32), inner.astype(jnp.int32))
    best = jnp.where((fits == 1) & (subset[0:1] < 16), subset[0:1], 16).astype(jnp.float32)
    best = jnp.min(best, axis=1, keepdims=True).astype(jnp.int32)
    picked = subset == best

    def at_best(x):
        return jnp.sum(jnp.where(picked, x, 0).astype(jnp.float32), axis=1, keepdims=True).astype(jnp.int32)

    go, right, left = at_best(chosen), at_best(right), at_best(left)

    def first_slots(x):
        starts = [jnp.zeros_like(x[0:1])]
        for i in range(3):
            starts.append(starts[i] + x[i : i + 1])
        starts[3] = jnp.where(turn, TURN, starts[3])
        return jnp.concatenate(starts, axis=0)

    return go, first_slots(right), first_slots(left)


def boundary_plan(ids_ref, blocks, planes, z, j):
    reach = 128 // 4
    count = ids_ref.shape[1] // 128
    blocks[...] = jnp.full(blocks.shape, -1, jnp.int32)
    for b in range(count):
        blocks[b + 1 : b + 2, :] = ids_ref[:, b * 128 : (b + 1) * 128]
    here, ahead, behind = [
        jnp.concatenate([blocks[pl.ds(4 * j + k + d, 1), :] for k in range(4)], axis=0) for d in (1, 2, 0)
    ]
    span = 128 // planes
    first_plane, last_plane = z == 0, z == planes - 1
    place = lax.broadcasted_iota(jnp.int32, (4, 128), 1)
    inside = place < reach

    def turned(x, plane):
        return pltpu.roll(x, lax.rem(2 * 128 - plane * span, 128), 1)

    own = turned(here, z)
    prior = turned(jnp.where(first_plane, behind, here), z - 1)
    later = turned(jnp.where(last_plane, ahead, here), z + 1)

    def matching(x, value, straddles):
        hits = jnp.sum(jnp.where(inside & (x == value), 1.0, 0.0), axis=1, keepdims=True)
        return jnp.where(straddles, hits, 0.0).astype(jnp.int32)

    first, last = own[:, 0:1], own[:, reach - 1 : reach]
    before, after = prior[:, reach - 1 : reach], later[:, 0:1]
    tail_r, head_r = [matching(x, last, last == after) for x in (own, later)]
    tail_l, head_l = [matching(x, first, first == before) for x in (prior, own)]
    go_r, right_r, left_r = directions(tail_r, head_r, last_plane)

    def shifted(x, by):
        rows = [x[(i + by) % 4 : (i + by) % 4 + 1] for i in range(4)]
        return jnp.where(first_plane, jnp.concatenate(rows, axis=0), x)

    go_l, right_l, left_l = [
        shifted(x, 3) for x in directions(shifted(tail_l, 1), shifted(head_l, 1), first_plane)
    ]
    sent_r, sent_l = jnp.where(go_r == 1, tail_r, 0), jnp.where(go_l == 0, head_l, 0)
    got_l, got_r = jnp.where(go_l == 1, tail_l, 0), jnp.where(go_r == 0, head_r, 0)
    begin = reach - sent_r
    slots = jnp.where(
        inside & (place >= begin),
        right_r + place - begin,
        jnp.where(place < sent_l, 48 + left_l + place, -1),
    )
    kept = jnp.where(slots >= 0, -1, own)
    lane = lax.broadcasted_iota(jnp.int32, (1, 128), 1)
    route = one_hot(lane // 32 * 8 + lane % 8, 0, (128, 128))
    block = lane // 8 % 4

    def arrival(x):
        moved = dot_nn(small(jnp.concatenate([x] * 4, axis=0)), route)
        total = jnp.zeros((1, 128), jnp.float32)
        for k in range(4):
            total = total + jnp.where(block == k, moved[k : k + 1], 0.0)
        return total.astype(jnp.int32)

    left_hit = (place >= right_l) & (place < right_l + got_l)
    right_hit = (place >= 48 + left_r) & (place < 48 + left_r + got_r)
    foreign = jnp.where(left_hit, first, jnp.where(right_hit, last, -1))
    foreign = jnp.max(foreign.astype(jnp.float32), axis=0, keepdims=True).astype(jnp.int32)
    return arrival(slots), arrival(kept), foreign


def kernel(
    group, planes, sections, chunks, width,
    q_ref, k_ref, v_ref, g_ref, packing_ref, ids_ref,
    out_ref,
    loaded, packed, win, halo, halo_in, back_out, back_in, fin_out, fin_in, unpack_in, bias, valid,
    pack_ref, unpack_ref, pick_ref, place_ref, blocks, load_s,
    a2a_s, a2a_r, halo_s, halo_r, back_s, back_r, fin_s, fin_r, un_s, un_r,
):
    t = lax.axis_index("section")
    me = lax.axis_index("dp")
    z, j = lax.div(me, group), lax.rem(me, group)
    rows = 128 // group
    before = lax.rem(t + sections - 1, sections)
    after = lax.rem(t + 1, sections)
    zr, zl = lax.rem(z + 1, planes), lax.rem(z + planes - 1, planes)
    jr = lax.rem(j + jnp.where(z == planes - 1, 1, 0), group)
    jl = lax.rem(j + group - jnp.where(z == 0, 1, 0), group)
    sides = (zr * group + j, zr * group + jr, zl * group + j, zl * group + jl)
    mates = [lax.rem(j + o, group) for o in range(group)]
    sources = [lax.rem(j + group - o, group) for o in range(group)]

    def columns(start):
        return pl.ds(pl.multiple_of(start, 128), CHUNK)

    def load(c, a):
        ref = (q_ref, k_ref, v_ref, g_ref)[a]
        return pltpu.make_async_copy(ref.at[0, :, columns(c * CHUNK)], loaded.at[c, a], load_s.at[c, a])

    @pl.loop(0, chunks)
    def _(c):
        for n in (5, 11):
            halo_in[c, n] = jnp.zeros(halo_in.shape[2:], jnp.bfloat16)
            back_in[c, n] = jnp.zeros(back_in.shape[2:], jnp.bfloat16)

    barrier = pltpu.get_barrier_semaphore()
    for o in range(1, group):
        pl.semaphore_signal(barrier, inc=1, device_id=(t, z * group + mates[o]), device_id_type=MESH)
    for side in sides:
        pl.semaphore_signal(barrier, inc=1, device_id=(t, side), device_id_type=MESH)
    for o in range(group):
        pl.semaphore_signal(barrier, inc=1, device_id=(after, z * group + mates[o]), device_id_type=MESH)

    @pl.loop(0, chunks)
    def _(c):
        for a in range(4):
            load(c, a).start()

    order = packing_ref[0]
    unpack_ref[...] = one_hot(order, 0, (128, 128))
    pack_ref[...] = one_hot(upright(order), 1, (128, 128))
    pl.semaphore_wait(barrier, 2 * group + 3)

    def at_rows(ref, c, start, count):
        if not isinstance(start, int):
            start = pl.multiple_of(start, 16)
        return ref.at[c, :, pl.ds(start, count), :]

    def a2a(c, o, landing):
        return pltpu.make_async_remote_copy(
            src_ref=at_rows(packed, c, mates[o] * rows, rows),
            dst_ref=at_rows(win, c, landing * rows, rows),
            send_sem=a2a_s.at[c, o - 1],
            recv_sem=a2a_r.at[c, o - 1],
            device_id=(t, z * group + mates[o]),
            device_id_type=MESH,
        )

    last_plane, first_plane = z == planes - 1, z == 0
    right_a, right_b, left_a, left_b = sides
    rightward = (((0, 5, 0, right_a),), ((0, 4, 0, right_a), (4, 2, 1, right_b)))
    leftward = (((6, 5, 2, left_a),), ((6, 4, 2, left_a), (10, 2, 3, left_b)))
    returned_left = (((0, 5, 0, left_a),), ((0, 4, 0, left_a), (4, 2, 1, left_b)))
    returned_right = (((6, 5, 2, right_a),), ((6, 4, 2, right_a), (10, 2, 3, right_b)))

    def each(copies, turn, act):
        for n in range(2):
            @pl.when(turn if n == 1 else jnp.logical_not(turn))
            def _():
                for copy in copies[n]:
                    act(*copy)

    def outward(c, act):
        def one(first, count, n, target):
            act(pltpu.make_async_remote_copy(
                src_ref=halo.at[c, pl.ds(first, count)],
                dst_ref=halo_in.at[c, pl.ds(first, count)],
                send_sem=halo_s.at[c, n],
                recv_sem=halo_r.at[c, n],
                device_id=(t, target),
                device_id_type=MESH,
            ))
        return one

    def homeward(c, act):
        def one(first, count, n, target):
            act(pltpu.make_async_remote_copy(
                src_ref=back_out.at[c, pl.ds(first, count)],
                dst_ref=back_in.at[c, pl.ds(first, count)],
                send_sem=back_s.at[c, n],
                recv_sem=back_r.at[c, n],
                device_id=(t, target),
                device_id_type=MESH,
            ))
        return one

    def start(copy):
        copy.start()

    def landed(copy):
        copy.wait_recv()

    def gone(copy):
        copy.wait_send()

    def outward_sends(c, act):
        each(rightward, last_plane, outward(c, act))
        each(leftward, first_plane, outward(c, act))

    def outward_arrivals(c):
        each(returned_left, first_plane, outward(c, landed))
        each(returned_right, last_plane, outward(c, landed))

    def homeward_sends(c, act):
        each(returned_left, first_plane, homeward(c, act))
        each(returned_right, last_plane, homeward(c, act))

    def homeward_arrivals(c):
        each(rightward, last_plane, homeward(c, landed))
        each(leftward, first_plane, homeward(c, landed))

    def final(c, o, landing):
        return pltpu.make_async_remote_copy(
            src_ref=at_rows(fin_out, c, mates[o] * rows, rows),
            dst_ref=at_rows(fin_in, c, landing * rows, rows),
            send_sem=fin_s.at[c, o],
            recv_sem=fin_r.at[c, o],
            device_id=(before, z * group + mates[o]),
            device_id_type=MESH,
        )

    unpack_copy = pltpu.make_async_remote_copy(
        src_ref=unpack_ref, dst_ref=unpack_in, send_sem=un_s, recv_sem=un_r,
        device_id=(before, me), device_id_type=MESH,
    )
    unpack_copy.start()

    lead = (2, 2, 4, 6, 8)

    def hand_out(c):
        for a in range(4):
            load(c, a).wait()
            packed[c, a] = dot_nn(pack_ref[...], loaded[c, a]).astype(jnp.bfloat16)
        for o in range(1, group):
            a2a(c, o, j).start()
        own = pl.ds(pl.multiple_of(j * rows, 16), rows)
        for a in range(4):
            win[c, a, own, :] = packed[c, a, own, :]
            win[c, a, 224:256, :] = jnp.zeros((32, CHUNK), jnp.bfloat16)

    @pl.loop(0, lead[0])
    def _(c):
        hand_out(c)

    slots, kept, foreign = boundary_plan(ids_ref, blocks, planes, z, j)
    pick_ref[...] = one_hot(slots, 0, (96, 128))
    place_ref[...] = one_hot(upright(slots), 1, (128, 96))
    id_row = jnp.concatenate([kept, foreign], axis=1)
    id_col = jnp.concatenate([upright(kept), upright(foreign)], axis=0)
    id_col = id_col[0:224]
    bias[...] = jnp.where((id_col == id_row) & (id_row >= 0), 0.0, NEG)
    valid[...] = jnp.where(id_col >= 0, 1.0, 0.0)
    scale = HEAD_DIM ** (-0.5)

    def spread(c):
        for o in range(1, group):
            a2a(c, o, sources[o]).wait_recv()
        picked = [
            dot_nn(pick_ref[...], win[c, a, 0:128, :]).reshape(GROUPS, 8, CHUNK) for a in range(4)
        ]
        for a in (0, 2):
            pair = jnp.concatenate(picked[a : a + 2], axis=1)
            halo[c, :, a * 8 : a * 8 + 16, :] = pair.astype(jnp.bfloat16)
        outward_sends(c, start)

    def attend(c):
        outward_arrivals(c)
        for a in (0, 2):
            pair = halo_in[c, :, a * 8 : a * 8 + 16, :].astype(jnp.float32)
            for n in range(2):
                cells = pair[:, n * 8 : n * 8 + 8].reshape(GROUPS * 8, CHUNK)
                win[c, a + n, 128:224, :] = cells.astype(jnp.bfloat16)
        foreign = []
        for h in range(CHUNK // HEAD_DIM):
            head = slice(h * HEAD_DIM, (h + 1) * HEAD_DIM)
            q, g = [win[c, a, 0:224, head] for a in (0, 3)]
            k, v = [win[c, a, :, head] for a in (1, 2)]
            s = dot_nt(q, k) * scale + bias[...]
            e = jnp.exp(s - jnp.max(s, axis=1, keepdims=True))
            p = e * (valid[...] / jnp.sum(e, axis=1, keepdims=True))
            low = p.astype(jnp.bfloat16)
            dp = dot_nt(g, v)
            delta = jnp.sum(low.astype(jnp.float32) * dp, axis=1, keepdims=True)
            ds = (p * (dp - delta) * scale).astype(jnp.bfloat16)
            for a, grad in enumerate((dot_nn(ds, k), dot_tn(ds, q), dot_tn(low, g))):
                fin_out[c, a, :, head] = grad[0:128].astype(jnp.bfloat16)
                foreign.append(grad[128:224].reshape(GROUPS, 8, HEAD_DIM))
                if len(foreign) % 2 == 0:
                    pair = jnp.concatenate(foreign[-2:], axis=1)
                    last = len(foreign) * 8
                    back_out[c, :, last - 16 : last, :] = pair.astype(jnp.bfloat16)
        homeward_sends(c, start)

    def hand_on(c):
        homeward_arrivals(c)
        foreign = []
        for n in range(0, 3 * CHUNK // HEAD_DIM, 2):
            pair = back_in[c, :, n * 8 : n * 8 + 16, :].astype(jnp.float32)
            for i in range(2):
                foreign.append(pair[:, i * 8 : i * 8 + 8].reshape(GROUPS * 8, HEAD_DIM))
        for a in range(3):
            returned = dot_nn(place_ref[...], jnp.concatenate(foreign[a::3], axis=1).astype(jnp.bfloat16))
            fin_out[c, a] = (fin_out[c, a].astype(jnp.float32) + returned).astype(jnp.bfloat16)
        for o in range(group):
            final(c, o, j).start()

    def finish(c):
        for o in range(group):
            final(c, o, sources[o]).wait_recv()
        for a in range(3):
            out_ref[0, :, columns(a * width + c * CHUNK)] = dot_nn(
                unpack_in[...], fin_in[c, a]
            ).astype(jnp.bfloat16)

    stages = (hand_out, spread, attend, hand_on, finish)

    @pl.loop(lead[0], chunks + lead[4])
    def _(step):
        @pl.when(step == lead[4])
        def _():
            unpack_copy.wait_recv()

        for n, stage in enumerate(stages):
            late = lead[n] if n > 0 else 0

            @pl.when((step >= late) & (step < chunks + late))
            def _():
                stage(step - late)

    unpack_copy.wait_send()

    @pl.loop(0, chunks)
    def _(c):
        for o in range(1, group):
            a2a(c, o, j).wait_send()
        outward_sends(c, gone)
        homeward_sends(c, gone)
        for o in range(group):
            final(c, o, j).wait_send()


def fused_body(sections, queries, key_cells, value_cells, grad_cells, packing, segment_ids):
    cell_count, width = queries.shape[1:]
    devices = lax.axis_size("dp")
    group = devices // 4
    planes = devices // group
    chunks = width // CHUNK
    vmem = pl.BlockSpec(memory_space=pltpu.VMEM)
    far = pl.BlockSpec(memory_space=pl.ANY)
    bf16 = jnp.bfloat16
    sem = pltpu.SemaphoreType.DMA
    return pl.pallas_call(
        functools.partial(kernel, group, planes, sections, chunks, width),
        out_shape=jax.ShapeDtypeStruct((1, cell_count, 3 * width), bf16),
        in_specs=[far] * 4 + [vmem] * 2,
        out_specs=vmem,
        scratch_shapes=[
            pltpu.VMEM((chunks, 4, 128, CHUNK), bf16),
            pltpu.VMEM((chunks, 4, 128, CHUNK), bf16),
            pltpu.VMEM((chunks, 4, 256, CHUNK), bf16),
            pltpu.VMEM((chunks, GROUPS, 32, CHUNK), bf16),
            pltpu.VMEM((chunks, GROUPS, 32, CHUNK), bf16),
            pltpu.VMEM((chunks, GROUPS, 24 * CHUNK // HEAD_DIM, HEAD_DIM), bf16),
            pltpu.VMEM((chunks, GROUPS, 24 * CHUNK // HEAD_DIM, HEAD_DIM), bf16),
            pltpu.VMEM((chunks, 3, 128, CHUNK), bf16),
            pltpu.VMEM((chunks, 3, 128, CHUNK), bf16),
            pltpu.VMEM((128, 128), bf16),
            pltpu.VMEM((224, 256), jnp.float32),
            pltpu.VMEM((224, 1), jnp.float32),
            pltpu.VMEM((128, 128), bf16),
            pltpu.VMEM((128, 128), bf16),
            pltpu.VMEM((96, 128), bf16),
            pltpu.VMEM((128, 96), bf16),
            pltpu.VMEM((segment_ids.shape[1] // 128 + 8, 128), jnp.int32),
            sem((chunks, 4)),
            sem((chunks, group - 1)), sem((chunks, group - 1)),
            sem((chunks, 4)), sem((chunks, 4)),
            sem((chunks, 4)), sem((chunks, 4)),
            sem((chunks, group)), sem((chunks, group)),
            sem, sem,
        ],
        compiler_params=pltpu.CompilerParams(
            collective_id=0, has_side_effects=True, vmem_limit_bytes=60 * 1024 * 1024
        ),
    )(queries, key_cells, value_cells, grad_cells, packing, segment_ids)


def solution(mesh):
    sections, devices = mesh.shape["section"], mesh.shape["dp"]

    def body_of(queries, *rest):
        fits = queries.shape[1] == 128 and queries.shape[2] % CHUNK == 0 and devices == 16
        if fits:
            return fused_body(sections, queries, *rest)
        return body(queries, *rest)

    return jax.shard_map(
        body_of,
        mesh=mesh,
        in_specs=(
            P("section", "dp", None),
            P("section", "dp", None),
            P("section", "dp", None),
            P("section", "dp", None),
            P("section", "dp", None),
            P("section", None),
        ),
        out_specs=P("section", "dp", None),
        check_vma=False,
    )
```

profile of v0, /device:TPU:0, one launch (start us, length us, event | category | flops | bytes accessed | tf_op | source)
XLA Modules:
  0.0 98.2 jit_solution(6382620949208957589)
XLA Ops:
  0.0 95.2 %shard_map.64 = bf16[1,128,7680]{2,1,0:T(8,128)(2,1)} custom-call(bf16[1,128,2560]{2,1,0:T(8,128)(2,1)} %q_ref.1, bf16[1,128,2560]{2,1,0:T(8,128)(2,1)} %k_ref.1, bf16[1,128,2560]{2,1,0:T(8,128)(2,1)} %v_ref.1, bf16[1,128,2560]{2,1,0:T(8,128)(2,1)} %g_ref.1, s32[1,1,128]{2,1,0:T(1,128)} %packing_ref.1, s32[1,2048]{1,0:T(1,128)} %ids_ref.1), custom_call_target="tpu_custom_call" | custom-call | tf_op jit(solution)/shard_map/pallas_call | solution.py:532
  95.2 2.9 %copy.8 = bf16[1,128,7680]{2,1,0:T(8,128)(2,1)} copy(bf16[1,128,7680]{2,1,0:T(8,128)(2,1)} %shard_map.64) | data formatting | bytes 3932160
where the time goes:
time: 98.4 us; the launch traced here: 98.2 us
  Pallas kernels  95.2 us (97%)
  local copies, waits for them, and re-layouts  2.94 us (3%)
    pallas_call x1, Pallas kernels, fused_body(): pl.pallas_call(functools.partial(kernel, group, planes, sections, chunks,...  95.2 us
    unnamed x1, local copies, waits for them, and re-layouts  2.94 us

commit v1 on v0

--- a/solution.py
+++ b/solution.py
@@ -262,8 +262,8 @@
 def kernel(
     group, planes, sections, chunks, width,
     q_ref, k_ref, v_ref, g_ref, packing_ref, ids_ref,
-    out_ref,
-    loaded, packed, win, halo, halo_in, back_out, back_in, fin_out, fin_in, unpack_in, bias, valid,
+    fin_in, unpack_in,
+    loaded, packed, win, halo, halo_in, back_out, back_in, fin_out, bias, valid,
     pack_ref, unpack_ref, pick_ref, place_ref, blocks, load_s,
     a2a_s, a2a_r, halo_s, halo_r, back_s, back_r, fin_s, fin_r, un_s, un_r,
 ):
@@ -293,6 +293,9 @@
             halo_in[c, n] = jnp.zeros(halo_in.shape[2:], jnp.bfloat16)
             back_in[c, n] = jnp.zeros(back_in.shape[2:], jnp.bfloat16)
 
+    for a in range(4):
+        load(0, a).start()
+
     barrier = pltpu.get_barrier_semaphore()
     for o in range(1, group):
         pl.semaphore_signal(barrier, inc=1, device_id=(t, z * group + mates[o]), device_id_type=MESH)
@@ -301,7 +304,7 @@
     for o in range(group):
         pl.semaphore_signal(barrier, inc=1, device_id=(after, z * group + mates[o]), device_id_type=MESH)
 
-    @pl.loop(0, chunks)
+    @pl.loop(1, chunks)
     def _(c):
         for a in range(4):
             load(c, a).start()
@@ -405,8 +408,6 @@
     )
     unpack_copy.start()
 
-    lead = (2, 2, 4, 6, 8)
-
     def hand_out(c):
         for a in range(4):
             load(c, a).wait()
@@ -418,7 +419,7 @@
             win[c, a, own, :] = packed[c, a, own, :]
             win[c, a, 224:256, :] = jnp.zeros((32, CHUNK), jnp.bfloat16)
 
-    @pl.loop(0, lead[0])
+    @pl.loop(0, 2)
     def _(c):
         hand_out(c)
 
@@ -484,30 +485,18 @@
         for o in range(group):
             final(c, o, j).start()
 
-    def finish(c):
-        for o in range(group):
-            final(c, o, sources[o]).wait_recv()
-        for a in range(3):
-            out_ref[0, :, columns(a * width + c * CHUNK)] = dot_nn(
-                unpack_in[...], fin_in[c, a]
-            ).astype(jnp.bfloat16)
-
-    stages = (hand_out, spread, attend, hand_on, finish)
-
-    @pl.loop(lead[0], chunks + lead[4])
+    stages = (spread, attend, hand_on, hand_out)
+    lead = (2, 4, 6, 0)
+
+    @pl.loop(2, chunks + max(lead))
     def _(step):
-        @pl.when(step == lead[4])
-        def _():
-            unpack_copy.wait_recv()
-
-        for n, stage in enumerate(stages):
-            late = lead[n] if n > 0 else 0
+        for late, stage in zip(lead, stages):
 
             @pl.when((step >= late) & (step < chunks + late))
             def _():
                 stage(step - late)
 
-    unpack_copy.wait_send()
+    unpack_copy.wait()
 
     @pl.loop(0, chunks)
     def _(c):
@@ -517,6 +506,14 @@
         homeward_sends(c, gone)
         for o in range(group):
             final(c, o, j).wait_send()
+            final(c, o, sources[o]).wait_recv()
+
+
+def put_in_place(unpack_ref, arrived_ref, out_ref):
+    chunks = arrived_ref.shape[0]
+    for c in range(chunks):
+        rows = dot_nn(unpack_ref[...], arrived_ref[c, 0])
+        out_ref[0, :, c * CHUNK : (c + 1) * CHUNK] = rows.astype(jnp.bfloat16)
 
 
 def fused_body(sections, queries, key_cells, value_cells, grad_cells, packing, segment_ids):
@@ -529,11 +526,14 @@
     far = pl.BlockSpec(memory_space=pl.ANY)
     bf16 = jnp.bfloat16
     sem = pltpu.SemaphoreType.DMA
-    return pl.pallas_call(
+    arrived, unpack = pl.pallas_call(
         functools.partial(kernel, group, planes, sections, chunks, width),
-        out_shape=jax.ShapeDtypeStruct((1, cell_count, 3 * width), bf16),
+        out_shape=(
+            jax.ShapeDtypeStruct((chunks, 3, cell_count, CHUNK), bf16),
+            jax.ShapeDtypeStruct((cell_count, cell_count), bf16),
+        ),
         in_specs=[far] * 4 + [vmem] * 2,
-        out_specs=vmem,
+        out_specs=(far, far),
         scratch_shapes=[
             pltpu.VMEM((chunks, 4, 128, CHUNK), bf16),
             pltpu.VMEM((chunks, 4, 128, CHUNK), bf16),
@@ -543,8 +543,6 @@
             pltpu.VMEM((chunks, GROUPS, 24 * CHUNK // HEAD_DIM, HEAD_DIM), bf16),
             pltpu.VMEM((chunks, GROUPS, 24 * CHUNK // HEAD_DIM, HEAD_DIM), bf16),
             pltpu.VMEM((chunks, 3, 128, CHUNK), bf16),
-            pltpu.VMEM((chunks, 3, 128, CHUNK), bf16),
-            pltpu.VMEM((128, 128), bf16),
             pltpu.VMEM((224, 256), jnp.float32),
             pltpu.VMEM((224, 1), jnp.float32),
             pltpu.VMEM((128, 128), bf16),
@@ -563,6 +561,17 @@
             collective_id=0, has_side_effects=True, vmem_limit_bytes=60 * 1024 * 1024
         ),
     )(queries, key_cells, value_cells, grad_cells, packing, segment_ids)
+    return pl.pallas_call(
+        put_in_place,
+        grid=(3,),
+        out_shape=jax.ShapeDtypeStruct((1, cell_count, 3 * width), bf16),
+        in_specs=[
+            pl.BlockSpec((cell_count, cell_count), lambda a: (0, 0)),
+            pl.BlockSpec((chunks, 1, cell_count, CHUNK), lambda a: (0, a, 0, 0)),
+        ],
+        out_specs=pl.BlockSpec((1, cell_count, width), lambda a: (0, 0, a)),
+        compiler_params=pltpu.CompilerParams(vmem_limit_bytes=60 * 1024 * 1024),
+    )(unpack, arrived)
 
 
 def solution(mesh):

time: 98.4 us -> 98 us (level)
  local copies, waits for them, and re-layouts: 2.94 us -> 0 us
  Pallas kernels: 95.2 us -> 97.7 us
    pallas_call x0 -> x1, Pallas kernels: none -> 4.16 us  [fused_body(): pl.pallas_call(put_in_place, grid=(3,), out_shape=jax.ShapeDtypeStruct((1...]
    unnamed x1 -> x0, local copies, waits for them, and re-layouts: 2.94 us -> none
    pallas_call x1, Pallas kernels: 95.2 us -> 93.6 us  [fused_body(): pl.pallas_call(functools.partial(kernel, group, planes, sections, chunks,...]
where the time goes in v1:
time: 98 us; the launch traced here: 97.7 us
  Pallas kernels  97.7 us (100%)
    pallas_call x1, Pallas kernels, fused_body(): pl.pallas_call(functools.partial(kernel, group, planes, sections, chunks,...  93.6 us
    pallas_call x1, Pallas kernels, fused_body(): pl.pallas_call(put_in_place, grid=(3,), out_shape=jax.ShapeDtypeStruct((1...  4.16 us

profile of v1, /device:TPU:0, one launch (start us, length us, event | category | flops | bytes accessed | tf_op | source)
XLA Modules:
  0.0 97.7 jit_solution(2250681844895863474)
XLA Ops:
  0.0 93.6 %shard_map.64 = (bf16[10,3,128,256]{3,2,1,0:T(8,128)(2,1)}, bf16[128,128]{1,0:T(8,128)(2,1)}) custom-call(bf16[1,128,2560]{2,1,0:T(8,128)(2,1)} %q_ref.1, bf16[1,128,2560]{2,1,0:T(8,128)(2,1)} %k_ref.1, bf16[1,128,2560]{2,1,0:T(8,128)(2,1)} %v_ref.1, bf16[1,128,2560]{2,1,0:T(8,128)(2,1)} %g_ref.1, s32[1,1,128]{2,1,0:T(1,128)} %packing_ref.1, s32[1,2048]{1,0:T(1,128)} %ids_ref.1), custom_call_target="tpu_custom_call" | custom-call | tf_op jit(solution)/shard_map/pallas_call | solution.py:529
  93.6 4.2 %shard_map.65 = bf16[1,128,7680]{2,1,0:T(8,128)(2,1)} custom-call(bf16[128,128]{1,0:T(8,128)(2,1)} %get-tuple-element.7.unpack_ref, bf16[10,3,128,256]{3,2,1,0:T(8,128)(2,1)} %get-tuple-element.8.arrived_ref), custom_call_target="tpu_custom_call" | custom-call | tf_op jit(solution)/shard_map/pallas_call | solution.py:564
